TPU v7x, 32 devices: a whole 2x2x4 slice. The times are simulated.
32 devices in a mesh: dp: 8 (over z, y), mp: 4 (over x, core).
Axes of the slice: x: 2, y: 2, z: 4, core: 2. Of those that a mesh axis runs over, the one named last changes fastest.
Arguments:
- tokens: bfloat16 [1536, 1152], P('dp'), may hold values from -6 to 6
- doc_lengths: int32 [16, 2], P('dp'), may hold values from 1 to 48, as said below
- cotangent: bfloat16 [1536, 1152], P('dp'), may hold values from -6 to 6
- query_weight: bfloat16 [1152, 1024], P('dp', 'mp'), may hold values from -0.1875 to 0.1875
- key_weight: bfloat16 [1152, 256], P('dp'), may hold values from -0.1875 to 0.1875
- value_weight: bfloat16 [1152, 256], P('dp'), may hold values from -0.1875 to 0.1875
- out_weight: bfloat16 [1024, 1152], P('mp', 'dp'), may hold values from -0.1875 to 0.1875
- gate_weight: bfloat16 [1152, 6912], P('dp', 'mp'), may hold values from -0.1875 to 0.1875
- up_weight: bfloat16 [1152, 6912], P('dp', 'mp'), may hold values from -0.1875 to 0.1875
- down_weight: bfloat16 [6912, 1152], P('mp', 'dp'), may hold values from -0.078125 to 0.078125
- pre_attn_gain: bfloat16 [1152], P('dp'), may hold values from 0.5 to 1.5
- post_attn_gain: bfloat16 [1152], P('dp'), may hold values from 0.5 to 1.5
- pre_ffn_gain: bfloat16 [1152], P('dp'), may hold values from 0.5 to 1.5
- post_ffn_gain: bfloat16 [1152], P('dp'), may hold values from 0.5 to 1.5
- query_gain: bfloat16 [256], P('dp'), may hold values from 0.5 to 1.5
- key_gain: bfloat16 [256], P('dp'), may hold values from 0.5 to 1.5
Outputs:
- mixed: bfloat16 [1536, 1152], P('dp')
- tokens_grad: float32 [1536, 1152], P('dp')
- query_grad: float32 [1152, 1024], P('dp', 'mp')
- key_grad: float32 [1152, 256], P('dp')
- value_grad: float32 [1152, 256], P('dp')
- out_grad: float32 [1024, 1152], P('mp', 'dp')
- gate_grad: float32 [1152, 6912], P('dp', 'mp')
- up_grad: float32 [1152, 6912], P('dp', 'mp')
- down_grad: float32 [6912, 1152], P('mp', 'dp')
- pre_attn_grad: float32 [1152], P('dp')
- post_attn_grad: float32 [1152], P('dp')
- pre_ffn_grad: float32 [1152], P('dp')
- post_ffn_grad: float32 [1152], P('dp')
- query_gain_grad: float32 [256], P('dp')
- key_gain_grad: float32 [256], P('dp')
Inputs may be any that keep to these rules, and one draw needn't show every extreme that they name: Row b of doc_lengths gives the 2 document lengths of buffer b, the buffers of one index of dp being 2 consecutive rows; the documents lie end to end from the buffer's first row, and the rows after them are padding.
All inputs are finite; a program needn't handle non-finite values.
Results may differ from a plain program's by a relative error of at most 0.019.
Values may be sent and summed in bfloat16 or wider, within the bound.
A program may use at most 128 MiB of HBM per device.

v0:
```python
import jax
import jax.numpy as jnp
from jax import lax
from jax.sharding import PartitionSpec as P

WINDOW = 512
EPSILON = 1e-06
THETA_BASE = 10000.0
NEGATIVE = -1e30


def matmul(left_op, right_op):
    return jnp.dot(left_op, right_op, preferred_element_type=jnp.float32)


def inner_rows(left_op, right_op):
    return lax.dot_general(
        left_op, right_op, (((0,), (0,)), ((), ())), preferred_element_type=jnp.float32
    )


def inner_cols(left_op, right_op):
    return lax.dot_general(
        left_op, right_op, (((1,), (1,)), ((), ())), preferred_element_type=jnp.float32
    )


def normed(values, factor):
    return values * lax.rsqrt(jnp.mean(values * values, axis=-1, keepdims=True) + EPSILON) * factor


def rotate(values, cosine, sine_table):
    half_width = values.shape[-1] // 2
    leading = values[..., :half_width]
    trailing = values[..., half_width:]
    return jnp.concatenate(
        [leading * cosine - trailing * sine_table, trailing * cosine + leading * sine_table],
        axis=-1,
    )


def layout(lengths, row_count):
    batches, docs = lengths.shape
    total = batches * row_count
    index = jnp.arange(total, dtype=jnp.int32)
    buffer = index // row_count
    inside = index % row_count
    order = jnp.arange(docs, dtype=jnp.int32)
    ends = jnp.sum(
        jnp.where(order[None, :, None] >= order[None, None, :], lengths[:, None, :], 0), axis=2
    )
    row_ends = jnp.repeat(ends, row_count, axis=0)
    row_lengths = jnp.repeat(lengths, row_count, axis=0)
    passed = inside[:, None] >= row_ends
    segment = jnp.sum(passed.astype(jnp.int32), axis=1)
    begins = jnp.sum(jnp.where(passed, row_lengths, 0), axis=1)
    position = inside - begins
    live_rows = (segment < docs).astype(jnp.float32)
    group = buffer * (docs + 1) + segment
    allowed = (
        (group[:, None] == group[None, :])
        & (index[None, :] <= index[:, None])
        & (index[:, None] - index[None, :] < WINDOW)
    )
    return (position, live_rows, allowed)


def angles(position, head_width):
    half_width = head_width // 2
    frequency = THETA_BASE ** (-2.0 * jnp.arange(half_width, dtype=jnp.float32) / head_width)
    turned = position.astype(jnp.float32)[:, None] * frequency[None, :]
    return (jnp.cos(turned), jnp.sin(turned))


def on_device(
    tokens,
    doc_lengths,
    cotangent,
    query_weight,
    key_weight,
    value_weight,
    out_weight,
    gate_weight,
    up_weight,
    down_weight,
    pre_attn_gain,
    post_attn_gain,
    pre_ffn_gain,
    post_ffn_gain,
    query_gain,
    key_gain,
):
    low = jnp.bfloat16
    full = jnp.float32
    dp = lax.axis_size("dp")
    mp = lax.axis_size("mp")
    shard = lax.axis_index("mp")
    rows, width = tokens.shape
    share = width // dp
    head_width = query_weight.shape[1]
    units = gate_weight.shape[1] // dp
    own_rows = rows // mp
    own = (shard * own_rows, own_rows)
    gain_head = query_gain.shape[0]
    gains = jnp.concatenate(
        [pre_attn_gain, post_attn_gain, pre_ffn_gain, post_ffn_gain, query_gain, key_gain]
    )
    block = jnp.concatenate([query_weight, key_weight, value_weight, out_weight.T], axis=1)
    gains_row = jnp.pad(gains, (0, block.shape[1] - gains.shape[0]))[None]
    packed = jnp.concatenate([block, jnp.pad(gains_row, ((0, 15), (0, 0)))], axis=0)
    packed = lax.all_gather(packed, "dp", axis=0, tiled=False)
    attn_w = packed[:, :share].reshape(width, 4 * head_width)
    qkv_w = attn_w[:, : 3 * head_width]
    out_wt = attn_w[:, 3 * head_width :]
    all_gains = packed[:, share].astype(full)
    gain_one, gain_two, gain_three, gain_four = (
        all_gains[:, i * share : (i + 1) * share].reshape(width) for i in range(4)
    )
    query_g = all_gains[:, 4 * share : 4 * share + gain_head].reshape(head_width)
    key_g = all_gains[:, 4 * share + gain_head : 4 * share + 2 * gain_head].reshape(head_width)
    ffn_block = jnp.stack([gate_weight, up_weight, down_weight.T], axis=0)
    ffn_block = ffn_block.reshape(3, share, dp, units).transpose(2, 1, 0, 3)
    ffn_block = ffn_block.reshape(dp, share, 3 * units)
    ffn_w = lax.all_to_all(ffn_block, "dp", split_axis=0, concat_axis=0, tiled=True)
    ffn_w = ffn_w.reshape(width, 3 * units)
    glu_w = ffn_w[:, : 2 * units]
    down_wt = ffn_w[:, 2 * units :]
    inputs = tokens.astype(full)
    position, live_rows, allowed = layout(doc_lengths, rows // doc_lengths.shape[0])
    cosine, sine_table = angles(position, head_width)
    normed_in = normed(inputs, gain_one).astype(low)
    projected = matmul(normed_in, qkv_w)
    query_pre = projected[:, :head_width]
    key_pre = projected[:, head_width : 2 * head_width]
    value_low = projected[:, 2 * head_width :].astype(low)
    query_low = rotate(normed(query_pre, query_g), cosine, sine_table).astype(low)
    key_low = rotate(normed(key_pre, key_g), cosine, sine_table).astype(low)
    score_scale = head_width ** (-0.5)
    scores = inner_cols(query_low, key_low) * score_scale
    scores = jnp.where(allowed, scores, NEGATIVE)
    row_peak = jnp.max(scores, axis=1, keepdims=True)
    raised = jnp.exp(scores - row_peak)
    attention = raised / jnp.sum(raised, axis=1, keepdims=True)
    attention_low = attention.astype(low)
    attended = matmul(attention_low, value_low).astype(low)
    attn_part = inner_cols(attended, out_wt).astype(low)
    attn_sum = lax.psum_scatter(attn_part, "mp", scatter_dimension=0, tiled=True).astype(full)
    inputs_own = lax.dynamic_slice_in_dim(tokens, *own, axis=0).astype(full)
    upstream = lax.dynamic_slice_in_dim(cotangent, *own, axis=0).astype(full)
    live = lax.dynamic_slice_in_dim(live_rows, *own, axis=0)[:, None]

    def post_norm(values, factor):
        return normed(values, factor) * live

    attn_out, back_two = jax.vjp(post_norm, attn_sum, gain_two)
    middle = inputs_own + attn_out
    normed_mid_own, back_three = jax.vjp(normed, middle, gain_three)
    normed_mid = lax.all_gather(normed_mid_own.astype(low), ("dp", "mp"), axis=0, tiled=True)
    glu_pre = matmul(normed_mid, glu_w)
    gate_proj = glu_pre[:, :units]
    up_proj = glu_pre[:, units:]

    def glu(gate_in, up_in):
        return jax.nn.gelu(gate_in, approximate=True) * up_in

    hidden_full, back_glu = jax.vjp(glu, gate_proj, up_proj)
    hidden = hidden_full.astype(low)
    ffn_part = inner_cols(hidden, down_wt).astype(low)
    ffn_sum = lax.psum_scatter(ffn_part, ("dp", "mp"), scatter_dimension=0, tiled=True).astype(full)
    ffn_out, back_four = jax.vjp(post_norm, ffn_sum, gain_four)
    mixed_own = (middle + ffn_out).astype(low)
    d_ffn_own, grad_four = back_four(upstream)
    d_ffn = lax.all_gather(d_ffn_own.astype(low), ("dp", "mp"), axis=0, tiled=True)
    grad_down_t = inner_rows(d_ffn, hidden)
    d_hidden = matmul(d_ffn, down_wt)
    d_gate, d_up = back_glu(d_hidden)
    d_glu = jnp.concatenate([d_gate.astype(low), d_up.astype(low)], axis=1)
    d_mid_part = inner_cols(d_glu, glu_w).astype(low)
    d_mid = lax.psum_scatter(d_mid_part, ("dp", "mp"), scatter_dimension=0, tiled=True).astype(full)
    grad_glu = inner_rows(normed_mid, d_glu)
    ffn_grad = jnp.concatenate([grad_glu, grad_down_t], axis=1).astype(low)
    ffn_grad = ffn_grad.reshape(dp, share, 3 * units)
    ffn_grad = lax.all_to_all(ffn_grad, "dp", split_axis=0, concat_axis=0, tiled=True)
    ffn_grad = ffn_grad.reshape(dp, share, 3, units).transpose(2, 1, 0, 3)
    ffn_grad = ffn_grad.reshape(3, share, dp * units).astype(full)
    d_mid_add, grad_three = back_three(d_mid)
    d_middle = upstream + d_mid_add
    d_attn_own, grad_two = back_two(d_middle)
    d_attn = lax.all_gather(d_attn_own.astype(low), "mp", axis=0, tiled=True)
    grad_out_t = inner_rows(d_attn, attended)
    d_attended = matmul(d_attn, out_wt).astype(low)
    d_value = inner_rows(attention_low, d_attended).astype(low)
    d_probs = inner_cols(d_attended, value_low)
    d_scores = attention * (d_probs - jnp.sum(attention * d_probs, axis=1, keepdims=True))
    d_scores = d_scores.astype(low)
    d_query_rot = matmul(d_scores, key_low) * score_scale
    d_key_rot = inner_rows(d_scores, query_low) * score_scale

    def turned(values, factor):
        return rotate(normed(values, factor), cosine, sine_table)

    _, back_query = jax.vjp(turned, query_pre, query_g)
    d_query_pre, grad_qgain = back_query(d_query_rot)
    _, back_key = jax.vjp(turned, key_pre, key_g)
    d_key_pre, grad_kgain = back_key(d_key_rot)
    d_qkv = jnp.concatenate([d_query_pre.astype(low), d_key_pre.astype(low), d_value], axis=1)
    d_in_part = inner_cols(d_qkv, qkv_w).astype(low)
    d_in = lax.psum_scatter(d_in_part, "mp", scatter_dimension=0, tiled=True).astype(full)
    grad_qkv = inner_rows(normed_in, d_qkv)
    _, back_one = jax.vjp(normed, inputs_own, gain_one)
    d_in_add, grad_one = back_one(d_in)
    tokens_grad_own = d_middle + d_in_add
    pieces = [
        g.reshape(dp, -1)
        for g in (grad_one, grad_two, grad_three, grad_four, grad_qgain, grad_kgain)
    ]
    gains_grad = jnp.concatenate(pieces, axis=1)
    gains_grad = jnp.pad(gains_grad, ((0, 0), (0, 4 * head_width - gains_grad.shape[1])))
    weights_grad = jnp.concatenate([grad_qkv, grad_out_t], axis=1).reshape(
        dp, share, 4 * head_width
    )
    owned = jnp.concatenate(
        [weights_grad, jnp.pad(gains_grad[:, None], ((0, 0), (0, 15), (0, 0)))], axis=1
    ).astype(low)
    owned = lax.psum_scatter(owned, "dp", scatter_dimension=0, tiled=True)[0].astype(full)
    shared = jnp.concatenate(
        [
            owned[:share, head_width : 3 * head_width].reshape(-1),
            owned[share, : 4 * share + 2 * gain_head],
        ]
    )
    shared = lax.psum(shared, "mp")
    kv_grad = shared[: 2 * share * head_width].reshape(share, 2 * head_width)
    gain_out = shared[2 * share * head_width :]
    mixed = lax.all_gather(mixed_own, "mp", axis=0, tiled=True)
    tokens_grad = lax.all_gather(tokens_grad_own.astype(low), "mp", axis=0, tiled=True).astype(full)
    return (
        mixed,
        tokens_grad,
        owned[:share, :head_width],
        kv_grad[:, :head_width],
        kv_grad[:, head_width:],
        owned[:share, 3 * head_width :].T,
        ffn_grad[0],
        ffn_grad[1],
        ffn_grad[2].T,
        gain_out[:share],
        gain_out[share : 2 * share],
        gain_out[2 * share : 3 * share],
        gain_out[3 * share : 4 * share],
        gain_out[4 * share : 4 * share + gain_head],
        gain_out[4 * share + gain_head :],
    )


def solution(mesh):
    placed = (
        P("dp", None),
        P("dp", None),
        P("dp", None),
        P("dp", "mp"),
        P("dp", None),
        P("dp", None),
        P("mp", "dp"),
        P("dp", "mp"),
        P("dp", "mp"),
        P("mp", "dp"),
        P("dp"),
        P("dp"),
        P("dp"),
        P("dp"),
        P("dp"),
        P("dp"),
    )
    return jax.shard_map(
        on_device,
        mesh=mesh,
        in_specs=placed,
        out_specs=(
            P("dp", None),
            P("dp", None),
            P("dp", "mp"),
            P("dp", None),
            P("dp", None),
            P("mp", "dp"),
            P("dp", "mp"),
            P("dp", "mp"),
            P("mp", "dp"),
            P("dp"),
            P("dp"),
            P("dp"),
            P("dp"),
            P("dp"),
            P("dp"),
        ),
        check_vma=False,
    )
```

profile of v0, /device:TPU:0, one launch (start us, length us, event | category | flops | bytes accessed | tf_op | source)
XLA Modules:
  0.0 653.2 jit_solution(11283578642979378089)
XLA Ops:
  7.2 4.1 concatenate.49
  11.3 1.8 fusion.25
  15.0 1.2 fusion.16
  16.2 54.4 %all-gather.9.cloned.1.call-done = bf16[1280,1024]{1,0:T(8,128)(2,1)} async-done(((bf16[160,1024]{1,0:T(8,128)(2,1)}), bf16[1280,1024]{1,0:T(8,128)(2,1)}) %all-gather.9.cloned.1.call-update) | async-done | bytes 2621456 | tf_op jit(solution)/shard_map/all_gather | solution.py:111
  71.6 2.1 slice.161
  78.5 1.1 convolution_convert_fusion.6
  80.0 19.5 %reduce-scatter.6.cloned.1.call-done = bf16[48,1152]{1,0:T(8,128)(2,1)} async-done(((bf16[192,1152]{1,0:T(8,128)(2,1)}), bf16[48,1152]{1,0:T(8,128)(2,1)}) %reduce-scatter.6.cloned.1.call-update) | async-done | bytes 110608 | tf_op jit(solution)/shard_map/reduce_scatter | solution.py:147
  101.1 1.2 multiply_reduce_fusion
  102.3 1.7 multiply_convert_fusion.2
  107.0 1.9 copy.61
  111.2 4.4 maximum_bitcast_fusion
  115.6 3.1 reshape.329
  118.8 61.1 %all_to_all.10 = bf16[8,144,648]{2,1,0:T(8,128)(2,1)S(1)} all-to-all(bf16[8,144,648]{2,1,0:T(8,128)(2,1)} %reshape.329), channel_id=1, replica_groups=mesh['dp'=8,'mp'=4] {'dp'}, dimensions={0} | all-to-all | bytes 2985984 | tf_op jit(solution)/shard_map/all_to_all | solution.py:124
  179.8 4.0 fusion.14
  183.8 1.5 copy-done.7
  185.8 3.3 convolution_convert_fusion
  189.9 100.5 %reduce-scatter.8.cloned.1.call-done = bf16[48,1152]{1,0:T(8,128)(2,1)} async-done(((bf16[1536,1152]{1,0:T(8,128)(2,1)}), bf16[48,1152]{1,0:T(8,128)(2,1)}) %reduce-scatter.8.cloned.1.call-update) | async-done | bytes 110608 | tf_op jit(solution)/shard_map/reduce_scatter | solution.py:169
  291.5 1.2 fusion.41
  292.6 1.7 fusion.44
  294.4 59.1 %all-gather.7.cloned.1.call-done = bf16[1536,1152]{1,0:T(8,128)(2,1)} async-done(((bf16[48,1152]{1,0:T(8,128)(2,1)}), bf16[1536,1152]{1,0:T(8,128)(2,1)}) %all-gather.7.cloned.1.call-update) | async-done | bytes 3538960 | tf_op jit(solution)/shard_map/all_gather | solution.py:173
  353.5 5.0 fusion.11
  359.3 4.2 convolution_convert_fusion.1
  363.8 101.8 %reduce-scatter.10.cloned.1.call-done = bf16[48,1152]{1,0:T(8,128)(2,1)} async-done(((bf16[1536,1152]{1,0:T(8,128)(2,1)}), bf16[48,1152]{1,0:T(8,128)(2,1)}) %reduce-scatter.10.cloned.1.call-update) | async-done | bytes 110608 | tf_op jit(solution)/shard_map/reduce_scatter | solution.py:179
  465.5 1.2 fusion.42
  466.8 2.0 fusion.39
  469.0 6.8 %all_gather.26 = bf16[192,1152]{1,0:T(8,128)(2,1)S(1)} all-gather(bf16[48,1152]{1,0:T(8,128)(2,1)S(1)} %fusion.45), channel_id=1, replica_groups=mesh['dp'=8,'mp'=4] {'mp'}, dimensions={0}, use_global_device_ids=true | all-gather | bytes 552960 | tf_op jit(solution)/shard_map/all_gather | solution.py:189
  478.3 1.5 convolution_convert_fusion.7
  480.1 1.4 convolution_convert_fusion.4
  481.9 1.8 convolution_convert_fusion.2
  483.7 1.7 pad_maximum_fusion
  485.4 2.9 copy.63
  488.3 11.8 %reduce-scatter.12.cloned.1.call-done = bf16[48,1152]{1,0:T(8,128)(2,1)} async-done(((bf16[192,1152]{1,0:T(8,128)(2,1)}), bf16[48,1152]{1,0:T(8,128)(2,1)}) %reduce-scatter.12.cloned.1.call-update) | async-done | bytes 110608 | tf_op jit(solution)/shard_map/reduce_scatter | solution.py:208
  500.0 1.2 fusion.43
  501.5 1.8 fusion.1
  503.4 3.1 convolution_convert_fusion.5
  506.7 4.1 convolution_convert_fusion.3
  512.1 61.5 %all_to_all.11 = bf16[8,144,648]{2,1,0:T(8,128)(2,1)S(1)} all-to-all(bf16[8,144,648]{2,1,0:T(8,128)(2,1)S(1)} %pad_maximum_fusion.1), channel_id=1, replica_groups=mesh['dp'=8,'mp'=4] {'dp'}, dimensions={0} | all-to-all | bytes 2985984 | tf_op jit(solution)/shard_map/all_to_all | solution.py:183
  573.6 4.9 reshape.342
  578.4 8.8 %fusion.116 = (f32[1,144,8,216]{3,0,1,2:T(1,128)S(1)}, f32[1,144,8,216]{3,0,1,2:T(1,128)S(1)}, f32[1,144,8,216]{3,0,1,2:T(1,128)S(1)}) fusion(f32[3,144,8,216]{3,0,1,2:T(4,128)} %bitcast.45), kind=kLoop, calls=%fused_computation.220 | loop fusion | bytes 5971968 | tf_op jit(solution)/shard_map/slice | solution.py:246
  587.9 1.4 squeeze.17
  590.0 1.4 squeeze.16
  592.2 1.4 squeeze.15
  593.6 6.7 %all_gather.24 = bf16[192,1152]{1,0:T(8,128)(2,1)S(1)} all-gather(bf16[48,1152]{1,0:T(8,128)(2,1)S(1)} %copy-done.18), channel_id=1, replica_groups=mesh['dp'=8,'mp'=4] {'mp'}, dimensions={0}, use_global_device_ids=true | all-gather | bytes 552960 | tf_op jit(solution)/shard_map/all_gather | solution.py:235
  601.4 6.8 %all_gather.27 = bf16[192,1152]{1,0:T(8,128)(2,1)S(1)} all-gather(bf16[48,1152]{1,0:T(8,128)(2,1)S(1)} %fusion.47), channel_id=1, replica_groups=mesh['dp'=8,'mp'=4] {'mp'}, dimensions={0}, use_global_device_ids=true | all-gather | bytes 552960 | tf_op jit(solution)/shard_map/all_gather | solution.py:236
  609.2 1.0 bitcast_convert_fusion
  611.9 29.4 %all-reduce.10.cloned.1.call-done = f32[74368]{0:T(1024)} async-done(((f32[74368]{0:T(1024)}), f32[74368]{0:T(1024)}) %all-reduce.10.cloned.1.call-update) | async-done | bytes 297488 | tf_op jit(solution)/shard_map/psum | solution.py:232
  643.1 1.3 fusion.117
  644.4 1.5 fusion.118
  (247 shorter events, 30.7 us)
Async XLA Ops:
  7.2 63.4 %all-gather.9.cloned.1.call-start = ((), (), s32[]{:S(2)}) async-start(), calls=%async_computation.15 | async-start | bytes 2949120 | tf_op jit(solution)/shard_map/all_gather | solution.py:111
  13.1 86.4 %reduce-scatter.6.cloned.1.call-start = ((), (), s32[]{:S(2)}) async-start(), calls=%async_computation.7 | async-start | bytes 552960 | tf_op jit(solution)/shard_map/reduce_scatter | solution.py:147
  15.0 60.9 %copy-start.57 = (f32[128]{0:T(128)}, f32[128]{0:T(128)S(1)}, u32[]{:S(2)}) copy-start(f32[128]{0:T(128)S(1)} %multiply_power_fusion) | copy-start | bytes 1540
  16.2 58.7 %copy-start.59 = (f32[192]{0:T(256)}, f32[192]{0:T(256)S(1)}, u32[]{:S(2)}) copy-start(f32[192]{0:T(256)S(1)} %add_rsqrt_fusion) | copy-start | bytes 2308
  16.2 59.7 %copy-start.45 = (f32[192]{0:T(256)}, f32[192]{0:T(256)S(1)}, u32[]{:S(2)}) copy-start(f32[192]{0:T(256)S(1)} %fusion.98) | copy-start | bytes 2308
  71.5 3.3 copy-start.6
  73.6 3.9 copy-start.4
  75.5 2.1 copy-start.1
  77.0 27.1 %copy-start.14 = (bf16[144,1728]{1,0:T(8,128)(2,1)S(1)}, bf16[144,1728]{1,0:T(8,128)(2,1)}, u32[]{:S(2)}) copy-start(bf16[144,1728]{1,0:T(8,128)(2,1)} %param.23) | copy-start | bytes 1492996
  79.7 100.1 %all-gather.5.cloned.1.call-start = ((), (), s32[]{:S(2)}) async-start(), calls=%async_computation.8 | async-start | bytes 3649536 | tf_op jit(solution)/shard_map/all_gather | solution.py:158
  79.8 25.3 %copy-start.33 = (f32[48]{0:T(128)}, f32[48]{0:T(128)S(1)}, u32[]{:S(2)}) copy-start(f32[48]{0:T(128)S(1)} %dynamic_slice.10) | copy-start | bytes 580
  101.1 4.0 copy-start.43
  101.1 4.9 copy-start.15
  102.3 2.8 copy-start.65
  102.3 2.8 copy-start.51
  104.1 186.4 %reduce-scatter.8.cloned.1.call-start = ((), (), s32[]{:S(2)}) async-start(), calls=%async_computation.9 | async-start | bytes 3649536 | tf_op jit(solution)/shard_map/reduce_scatter | solution.py:169
  106.0 2.9 copy-start.16
  183.8 1.5 copy-start.7
  189.1 102.3 %copy-start.21 = (bf16[192,1152]{1,0:T(8,128)(2,1)S(1)}, bf16[192,1152]{1,0:T(8,128)(2,1)}, u32[]{:S(2)}) copy-start(bf16[192,1152]{1,0:T(8,128)(2,1)} %param.18) | copy-start | bytes 1327108
  189.1 102.3 %copy-start.34 = (f32[48]{0:T(128)S(1)}, f32[48]{0:T(128)}, u32[]{:S(2)}) copy-start(f32[48]{0:T(128)} %copy-done.33) | copy-start | bytes 580
  189.1 164.3 %all-gather.7.cloned.1.call-start = ((), (), s32[]{:S(2)}) async-start(), calls=%async_computation.10 | async-start | bytes 3649536 | tf_op jit(solution)/shard_map/all_gather | solution.py:173
  294.4 171.2 %reduce-scatter.10.cloned.1.call-start = ((), (), s32[]{:S(2)}) async-start(), calls=%async_computation.11 | async-start | bytes 3649536 | tf_op jit(solution)/shard_map/reduce_scatter | solution.py:179
  358.5 5.0 copy-start.68
  363.5 102.0 %copy-start.3 = (bf16[48,1152]{1,0:T(8,128)(2,1)S(1)}, bf16[48,1152]{1,0:T(8,128)(2,1)}, u32[]{:S(2)}) copy-start(bf16[48,1152]{1,0:T(8,128)(2,1)} %reduce-scatter.6.cloned.1.call-done) | copy-start | bytes 331780
  363.5 102.0 %copy-start.44 = (f32[48]{0:T(128)S(1)}, f32[48]{0:T(128)}, u32[]{:S(2)}) copy-start(f32[48]{0:T(128)} %copy-done.43) | copy-start | bytes 580
  363.5 102.0 %copy-start.52 = (f32[48]{0:T(128)S(1)}, f32[48]{0:T(128)}, u32[]{:S(2)}) copy-start(f32[48]{0:T(128)} %copy-done.51) | copy-start | bytes 580
  363.5 103.3 %copy-start.66 = (f32[48]{0:T(128)S(1)}, f32[48]{0:T(128)}, u32[]{:S(2)}) copy-start(f32[48]{0:T(128)} %copy-done.65) | copy-start | bytes 580
  363.5 103.3 %copy-start.11 = (bf16[48,1152]{1,0:T(8,128)(2,1)S(1)}, bf16[48,1152]{1,0:T(8,128)(2,1)}, u32[]{:S(2)}) copy-start(bf16[48,1152]{1,0:T(8,128)(2,1)} %reduce-scatter.8.cloned.1.call-done) | copy-start | bytes 331780
  363.6 105.3 %copy-start.64 = (f32[48]{0:T(128)S(1)}, f32[48]{0:T(128)}, u32[]{:S(2)}) copy-start(f32[48]{0:T(128)} %copy-done.63) | copy-start | bytes 580
  363.6 112.3 %copy-start.5 = (bf16[8,144,1024]{2,1,0:T(8,128)(2,1)S(1)}, bf16[8,144,1024]{2,1,0:T(8,128)(2,1)}, u32[]{:S(2)}) copy-start(bf16[8,144,1024]{2,1,0:T(8,128)(2,1)} %copy-done.4) | copy-start | bytes 7077892
  363.6 136.5 %reduce-scatter.12.cloned.1.call-start = ((), (), s32[]{:S(2)}) async-start(), calls=%async_computation.12 | async-start | bytes 552960 | tf_op jit(solution)/shard_map/reduce_scatter | solution.py:208
  363.7 112.5 %copy-start.13 = (f32[192,192]{0,1:T(8,128)S(1)}, f32[192,192]{0,1:T(8,128)}, u32[]{:S(2)}) copy-start(f32[192,192]{0,1:T(8,128)} %copy-done.12) | copy-start | bytes 442372
  363.7 112.5 %copy-start.54 = (f32[192]{0:T(256)S(1)}, f32[192]{0:T(256)}, u32[]{:S(2)}) copy-start(f32[192]{0:T(256)} %copy-done.53) | copy-start | bytes 2308
  363.8 112.5 %copy-start.56 = (f32[192]{0:T(256)S(1)}, f32[192]{0:T(256)}, u32[]{:S(2)}) copy-start(f32[192]{0:T(256)} %copy-done.55) | copy-start | bytes 2308
  466.8 21.5 %copy-start.61 = (f32[48]{0:T(128)}, f32[48]{0:T(128)S(1)}, u32[]{:S(2)}) copy-start(f32[48]{0:T(128)S(1)} %get-tuple-element.29) | copy-start | bytes 580
  468.9 7.9 %copy-start.8 = (f32[48,1152]{1,0:T(8,128)}, f32[48,1152]{1,0:T(8,128)S(1)}, u32[]{:S(2)}) copy-start(f32[48,1152]{1,0:T(8,128)S(1)} %get-tuple-element.34) | copy-start | bytes 663556
  468.9 7.6 %copy-start.2 = (f32[192,768]{1,0:T(8,128)S(1)}, f32[192,768]{1,0:T(8,128)}, u32[]{:S(2)}) copy-start(f32[192,768]{1,0:T(8,128)} %copy-done.1) | copy-start | bytes 1769476
  476.5 1.8 copy-start.67
  478.3 1.8 copy-start.20
  478.3 3.6 copy-start.31
  478.3 3.6 copy-start.60
  479.9 129.4 %reduce-scatter.14.cloned.1.call-start = ((), (), s32[]{:S(2)}) async-start(), calls=%async_computation.13 | async-start | bytes 2949120 | tf_op jit(solution)/shard_map/reduce_scatter | solution.py:225
  503.3 3.4 copy-start.69
  503.3 138.0 %all-reduce.10.cloned.1.call-start = ((), (), s32[]{:S(2)}) async-start(), calls=%async_computation.14 | async-start | bytes 598016 | tf_op jit(solution)/shard_map/psum | solution.py:232
  591.5 2.2 copy-start.18
  592.2 8.2 %copy-start.62 = (f32[48]{0:T(128)S(1)}, f32[48]{0:T(128)}, u32[]{:S(2)}) copy-start(f32[48]{0:T(128)} %copy-done.61) | copy-start | bytes 580
  592.2 8.2 %copy-start.9 = (f32[48,1152]{1,0:T(8,128)S(1)}, f32[48,1152]{1,0:T(8,128)}, u32[]{:S(2)}) copy-start(f32[48,1152]{1,0:T(8,128)} %copy-done.8) | copy-start | bytes 663556
  592.2 8.2 %copy-start.17 = (bf16[48,1152]{1,0:T(8,128)(2,1)S(1)}, bf16[48,1152]{1,0:T(8,128)(2,1)}, u32[]{:S(2)}) copy-start(bf16[48,1152]{1,0:T(8,128)(2,1)} %reduce-scatter.12.cloned.1.call-done) | copy-start | bytes 331780
  (32 other events, 31.8 us)
Sparse Core Ops, SparseCore 0:
  13.2 57.3 all-gather.8
  79.8 19.6 reduce-scatter.5
  104.2 70.9 all-gather.4
  189.3 101.1 reduce-scatter.7
  294.5 58.9 all-gather.6
  363.7 101.7 reduce-scatter.9
  480.0 20.0 reduce-scatter.11
  503.6 93.4 reduce-scatter.13
  611.3 29.9 all-reduce.9
where the time goes:
time: 654 us; the launch traced here: 653 us
  waiting for transfers between devices  377 us (58%)
  blocking collectives  143 us (22%)
  local copies, waits for them, and re-layouts  54 us (8%)
  other arithmetic  32.3 us (5%)
  matrix products  31.6 us (5%)
  between operations  15.1 us (2%)
    reduce_scatter x1, waiting for transfers between devices, on_device(): lax.psum_scatter(d_mid_part, ('dp', 'mp'), scatter_dimension=0, tiled=True)  102 us
    reduce_scatter x1, waiting for transfers between devices, on_device(): lax.psum_scatter(ffn_part, ('dp', 'mp'), scatter_dimension=0, tiled=True)  101 us
    all_to_all x1, blocking collectives, on_device(): lax.all_to_all(ffn_grad, 'dp', split_axis=0, concat_axis=0, tiled=True)  61.5 us
    all_to_all x1, blocking collectives, on_device(): lax.all_to_all(ffn_block, 'dp', split_axis=0, concat_axis=0, tiled=True)  61.1 us
    all_gather x1, waiting for transfers between devices, on_device(): lax.all_gather(d_ffn_own.astype(low), ('dp', 'mp'), axis=0, tiled=True)  59.1 us
    all_gather x1, waiting for transfers between devices, on_device(): packed = lax.all_gather(packed, 'dp', axis=0, tiled=False)  54.4 us
    psum x1, waiting for transfers between devices, on_device(): shared = lax.psum(shared, 'mp')  29.4 us
    reduce_scatter x1, waiting for transfers between devices, on_device(): lax.psum_scatter(attn_part, 'mp', scatter_dimension=0, tiled=True)  19.5 us
  transfers between devices with their start and end apart: 9, of which 7 were waited for; matrix products, arithmetic and copies ran while one was open for 9% of the time, Pallas kernels for 0%

commit v1 on v0

--- a/solution.py
+++ b/solution.py
@@ -121,7 +121,20 @@
     ffn_block = jnp.stack([gate_weight, up_weight, down_weight.T], axis=0)
     ffn_block = ffn_block.reshape(3, share, dp, units).transpose(2, 1, 0, 3)
     ffn_block = ffn_block.reshape(dp, share, 3 * units)
-    ffn_w = lax.all_to_all(ffn_block, "dp", split_axis=0, concat_axis=0, tiled=True)
+    heard, all_values = (lax.axis_size("dp"), lax.axis_index("dp"))
+    block_out = ffn_block.shape[0] // heard
+    b_next = list(ffn_block.shape)
+    b_next[0] = block_out
+    prior = b_next[0]
+    b_next[0] = prior * heard
+    ffn_w = jnp.zeros(b_next, ffn_block.dtype)
+    for ix in range(heard):
+        item_now = lax.dynamic_slice_in_dim(
+            ffn_block, (all_values ^ ix) * block_out, block_out, axis=0
+        )
+        if ix:
+            item_now = lax.ppermute(item_now, "dp", [(kk, kk ^ ix) for kk in range(heard)])
+        ffn_w = lax.dynamic_update_slice_in_dim(ffn_w, item_now, (all_values ^ ix) * prior, axis=0)
     ffn_w = ffn_w.reshape(width, 3 * units)
     glu_w = ffn_w[:, : 2 * units]
     down_wt = ffn_w[:, 2 * units :]

time: 654 us -> 661 us (1.011)
  blocking collectives: 143 us -> 81.6 us
  waiting for transfers between devices: 377 us -> 420 us
  starting transfers between devices: 0.59 us -> 16.1 us
    all_to_all x1 -> x0, blocking collectives: 61.1 us -> none  [on_device(): lax.all_to_all(ffn_block, 'dp', split_axis=0, concat_axis=0, tiled=True)]
    ppermute x0 -> x7, waiting for transfers between devices: none -> 42.4 us  [on_device(): lax.ppermute(item_now, 'dp', [(kk, kk ^ ix) for kk in range(heard)])]
    ppermute x0 -> x7, starting transfers between devices: none -> 15.3 us  [on_device(): lax.ppermute(item_now, 'dp', [(kk, kk ^ ix) for kk in range(heard)])]
  transfers between devices with their start and end apart: 9 -> 16, of which waited for: 7 -> 10; matrix products, arithmetic and copies ran while one was open for 9% -> 9% of each run, Pallas kernels for 0% -> 0%
where the time goes in v1:
time: 661 us; the launch traced here: 654 us
  waiting for transfers between devices  420 us (64%)
  blocking collectives  81.6 us (12%)
  local copies, waits for them, and re-layouts  56.3 us (9%)
  other arithmetic  33.2 us (5%)
  matrix products  31.6 us (5%)
  starting transfers between devices  16.1 us (2%)
  between operations  15.6 us (2%)
    reduce_scatter x1, waiting for transfers between devices, on_device(): lax.psum_scatter(ffn_part, ('dp', 'mp'), scatter_dimension=0, tiled=True)  101 us
    reduce_scatter x1, waiting for transfers between devices, on_device(): lax.psum_scatter(d_mid_part, ('dp', 'mp'), scatter_dimension=0, tiled=True)  101 us
    all_to_all x1, blocking collectives, on_device(): lax.all_to_all(ffn_grad, 'dp', split_axis=0, concat_axis=0, tiled=True)  61.3 us
    all_gather x1, waiting for transfers between devices, on_device(): lax.all_gather(d_ffn_own.astype(low), ('dp', 'mp'), axis=0, tiled=True)  58.9 us
    all_gather x1, waiting for transfers between devices, on_device(): packed = lax.all_gather(packed, 'dp', axis=0, tiled=False)  54.4 us
    ppermute x7, waiting for transfers between devices, on_device(): lax.ppermute(item_now, 'dp', [(kk, kk ^ ix) for kk in range(heard)])  42.4 us
    psum x1, waiting for transfers between devices, on_device(): shared = lax.psum(shared, 'mp')  29.4 us
    reduce_scatter x1, waiting for transfers between devices, on_device(): lax.psum_scatter(attn_part, 'mp', scatter_dimension=0, tiled=True)  19.5 us
  transfers between devices with their start and end apart: 16, of which 10 were waited for; matrix products, arithmetic and copies ran while one was open for 9% of the time, Pallas kernels for 0%

profile of v1, /device:TPU:0, one launch (start us, length us, event | category | flops | bytes accessed | tf_op | source)
XLA Modules:
  0.0 654.0 jit_solution(6159182421417925014)
XLA Ops:
  7.2 4.1 concatenate.49
  11.3 1.8 fusion.25
  16.2 54.4 %all-gather.9.cloned.1.call-done = bf16[1280,1024]{1,0:T(8,128)(2,1)} async-done(((bf16[160,1024]{1,0:T(8,128)(2,1)}), bf16[1280,1024]{1,0:T(8,128)(2,1)}) %all-gather.9.cloned.1.call-update) | async-done | bytes 2621456 | tf_op jit(solution)/shard_map/all_gather | solution.py:111
  71.6 2.1 slice.161
  80.0 19.5 %reduce-scatter.6.cloned.1.call-done = bf16[48,1152]{1,0:T(8,128)(2,1)} async-done(((bf16[192,1152]{1,0:T(8,128)(2,1)}), bf16[48,1152]{1,0:T(8,128)(2,1)}) %reduce-scatter.6.cloned.1.call-update) | async-done | bytes 110608 | tf_op jit(solution)/shard_map/reduce_scatter | solution.py:160
  102.3 1.7 multiply_convert_fusion.2
  107.0 1.9 copy.61
  111.2 4.9 maximum_bitcast_fusion
  116.1 3.1 reshape.329
  120.8 1.5 collective-permute-start
  122.3 1.5 collective-permute-start.1
  123.8 2.4 collective-permute-start.6
  126.2 1.5 collective-permute-start.5
  127.6 1.5 collective-permute-start.4
  129.1 6.9 %collective-permute-start.2 = (bf16[1,144,648]{2,1,0:T(8,128)(2,1)S(1)}, bf16[1,144,648]{2,1,0:T(8,128)(2,1)S(1)}, u32[]{:S(2)}, u32[]{:S(2)}) collective-permute-start(bf16[1,144,648]{2,1,0:T(8,128)(2,1)S(1)} %get-tuple-element.44), channel_id=1, source_target_pairs={{0,12},{4,8},{8,4},{12,0},{16,28},{20,24},{24,20},{28,16},{1,13},{... | collective-permute-start | bytes 559880 | tf_op jit(solution)/shard_map/ppermute | solution.py:136
  136.2 17.7 %collective-permute-done.2 = bf16[1,144,648]{2,1,0:T(8,128)(2,1)S(1)} collective-permute-done((bf16[1,144,648]{2,1,0:T(8,128)(2,1)S(1)}, bf16[1,144,648]{2,1,0:T(8,128)(2,1)S(1)}, u32[]{:S(2)}, u32[]{:S(2)}) %collective-permute-start.2) | collective-permute-done | bytes 186656 | tf_op jit(solution)/shard_map/ppermute | solution.py:136
  153.9 24.6 %collective-permute-done.3 = bf16[1,144,648]{2,1,0:T(8,128)(2,1)S(1)} collective-permute-done((bf16[1,144,648]{2,1,0:T(8,128)(2,1)S(1)}, bf16[1,144,648]{2,1,0:T(8,128)(2,1)S(1)}, u32[]{:S(2)}, u32[]{:S(2)}) %collective-permute-start.3) | collective-permute-done | bytes 186656 | tf_op jit(solution)/shard_map/ppermute | solution.py:136
  179.0 3.9 fusion.14
  183.0 1.5 copy-done.8
  185.0 3.3 convolution_convert_fusion
  189.1 101.3 %reduce-scatter.8.cloned.1.call-done = bf16[48,1152]{1,0:T(8,128)(2,1)} async-done(((bf16[1536,1152]{1,0:T(8,128)(2,1)}), bf16[48,1152]{1,0:T(8,128)(2,1)}) %reduce-scatter.8.cloned.1.call-update) | async-done | bytes 110608 | tf_op jit(solution)/shard_map/reduce_scatter | solution.py:182
  291.5 1.7 fusion.41
  293.1 1.7 fusion.44
  295.1 58.9 %all-gather.7.cloned.1.call-done = bf16[1536,1152]{1,0:T(8,128)(2,1)} async-done(((bf16[48,1152]{1,0:T(8,128)(2,1)}), bf16[1536,1152]{1,0:T(8,128)(2,1)}) %all-gather.7.cloned.1.call-update) | async-done | bytes 3538960 | tf_op jit(solution)/shard_map/all_gather | solution.py:186
  354.0 5.0 fusion.11
  360.0 4.2 convolution_convert_fusion.1
  365.0 101.1 %reduce-scatter.10.cloned.1.call-done = bf16[48,1152]{1,0:T(8,128)(2,1)} async-done(((bf16[1536,1152]{1,0:T(8,128)(2,1)}), bf16[48,1152]{1,0:T(8,128)(2,1)}) %reduce-scatter.10.cloned.1.call-update) | async-done | bytes 110608 | tf_op jit(solution)/shard_map/reduce_scatter | solution.py:192
  467.5 2.0 fusion.39
  469.7 6.8 %all_gather.26 = bf16[192,1152]{1,0:T(8,128)(2,1)S(1)} all-gather(bf16[48,1152]{1,0:T(8,128)(2,1)S(1)} %fusion.45), channel_id=1, replica_groups=mesh['dp'=8,'mp'=4] {'mp'}, dimensions={0}, use_global_device_ids=true | all-gather | bytes 552960 | tf_op jit(solution)/shard_map/all_gather | solution.py:202
  478.9 1.5 convolution_convert_fusion.7
  480.5 1.4 convolution_convert_fusion.4
  482.3 1.8 convolution_convert_fusion.2
  484.1 1.7 pad_maximum_fusion
  485.8 2.9 copy.63
  488.7 12.0 %reduce-scatter.12.cloned.1.call-done = bf16[48,1152]{1,0:T(8,128)(2,1)} async-done(((bf16[192,1152]{1,0:T(8,128)(2,1)}), bf16[48,1152]{1,0:T(8,128)(2,1)}) %reduce-scatter.12.cloned.1.call-update) | async-done | bytes 110608 | tf_op jit(solution)/shard_map/reduce_scatter | solution.py:221
  502.1 1.8 fusion.1
  504.2 3.0 convolution_convert_fusion.5
  507.5 4.1 convolution_convert_fusion.3
  512.9 61.3 %all_to_all.5 = bf16[8,144,648]{2,1,0:T(8,128)(2,1)S(1)} all-to-all(bf16[8,144,648]{2,1,0:T(8,128)(2,1)S(1)} %pad_maximum_fusion.1), channel_id=1, replica_groups=mesh['dp'=8,'mp'=4] {'dp'}, dimensions={0} | all-to-all | bytes 2985984 | tf_op jit(solution)/shard_map/all_to_all | solution.py:196
  574.2 4.8 reshape.342
  579.0 8.8 %fusion.116 = (f32[1,144,8,216]{3,0,1,2:T(1,128)S(1)}, f32[1,144,8,216]{3,0,1,2:T(1,128)S(1)}, f32[1,144,8,216]{3,0,1,2:T(1,128)S(1)}) fusion(f32[3,144,8,216]{3,0,1,2:T(4,128)} %bitcast.45), kind=kLoop, calls=%fused_computation.235 | loop fusion | bytes 5971968 | tf_op jit(solution)/shard_map/slice | solution.py:259
  588.5 1.4 squeeze.17
  590.6 1.4 squeeze.16
  592.8 1.4 squeeze.15
  594.2 6.7 %all_gather.24 = bf16[192,1152]{1,0:T(8,128)(2,1)S(1)} all-gather(bf16[48,1152]{1,0:T(8,128)(2,1)S(1)} %copy-done.19), channel_id=1, replica_groups=mesh['dp'=8,'mp'=4] {'mp'}, dimensions={0}, use_global_device_ids=true | all-gather | bytes 552960 | tf_op jit(solution)/shard_map/all_gather | solution.py:248
  602.0 6.8 %all_gather.27 = bf16[192,1152]{1,0:T(8,128)(2,1)S(1)} all-gather(bf16[48,1152]{1,0:T(8,128)(2,1)S(1)} %fusion.47), channel_id=1, replica_groups=mesh['dp'=8,'mp'=4] {'mp'}, dimensions={0}, use_global_device_ids=true | all-gather | bytes 552960 | tf_op jit(solution)/shard_map/all_gather | solution.py:249
  612.5 29.4 %all-reduce.10.cloned.1.call-done = f32[74368]{0:T(1024)} async-done(((f32[74368]{0:T(1024)}), f32[74368]{0:T(1024)}) %all-reduce.10.cloned.1.call-update) | async-done | bytes 297488 | tf_op jit(solution)/shard_map/psum | solution.py:245
  645.0 1.5 fusion.118
  (283 shorter events, 42.0 us)
Async XLA Ops:
  7.2 63.4 %all-gather.9.cloned.1.call-start = ((), (), s32[]{:S(2)}) async-start(), calls=%async_computation.14 | async-start | bytes 2949120 | tf_op jit(solution)/shard_map/all_gather | solution.py:111
  13.1 86.4 %reduce-scatter.6.cloned.1.call-start = ((), (), s32[]{:S(2)}) async-start(), calls=%async_computation.6 | async-start | bytes 552960 | tf_op jit(solution)/shard_map/reduce_scatter | solution.py:160
  15.0 60.9 %copy-start.64 = (f32[128]{0:T(128)}, f32[128]{0:T(128)S(1)}, u32[]{:S(2)}) copy-start(f32[128]{0:T(128)S(1)} %multiply_power_fusion) | copy-start | bytes 1540
  16.2 58.6 %copy-start.66 = (f32[192]{0:T(256)}, f32[192]{0:T(256)S(1)}, u32[]{:S(2)}) copy-start(f32[192]{0:T(256)S(1)} %add_rsqrt_fusion) | copy-start | bytes 2308
  16.2 59.7 %copy-start.50 = (f32[192]{0:T(256)}, f32[192]{0:T(256)S(1)}, u32[]{:S(2)}) copy-start(f32[192]{0:T(256)S(1)} %fusion.98) | copy-start | bytes 2308
  73.6 3.9 copy-start.5
  76.9 27.1 %copy-start.15 = (bf16[144,1728]{1,0:T(8,128)(2,1)S(1)}, bf16[144,1728]{1,0:T(8,128)(2,1)}, u32[]{:S(2)}) copy-start(bf16[144,1728]{1,0:T(8,128)(2,1)} %param.23) | copy-start | bytes 1492996
  79.6 99.4 %all-gather.5.cloned.1.call-start = ((), (), s32[]{:S(2)}) async-start(), calls=%async_computation.7 | async-start | bytes 3649536 | tf_op jit(solution)/shard_map/all_gather | solution.py:171
  79.8 25.3 %copy-start.36 = (f32[48]{0:T(128)}, f32[48]{0:T(128)S(1)}, u32[]{:S(2)}) copy-start(f32[48]{0:T(128)S(1)} %dynamic_slice.34) | copy-start | bytes 580
  101.1 4.0 copy-start.48
  101.1 4.9 copy-start.16
  104.0 186.4 %reduce-scatter.8.cloned.1.call-start = ((), (), s32[]{:S(2)}) async-start(), calls=%async_computation.8 | async-start | bytes 3649536 | tf_op jit(solution)/shard_map/reduce_scatter | solution.py:182
  120.8 8.4 %collective-permute-start = (bf16[1,144,648]{2,1,0:T(8,128)(2,1)S(1)}, bf16[1,144,648]{2,1,0:T(8,128)(2,1)S(1)}, u32[]{:S(2)}, u32[]{:S(2)}) collective-permute-start(bf16[1,144,648]{2,1,0:T(8,128)(2,1)S(1)} %get-tuple-element.46), channel_id=1, source_target_pairs={{0,4},{4,0},{8,12},{12,8},{16,20},{20,16},{24,28},{28,24},{1,5},{5... | collective-permute-start | bytes 559880 | tf_op jit(solution)/shard_map/ppermute | solution.py:136
  122.3 13.8 %collective-permute-start.1 = (bf16[1,144,648]{2,1,0:T(8,128)(2,1)S(1)}, bf16[1,144,648]{2,1,0:T(8,128)(2,1)S(1)}, u32[]{:S(2)}, u32[]{:S(2)}) collective-permute-start(bf16[1,144,648]{2,1,0:T(8,128)(2,1)S(1)} %get-tuple-element.45), channel_id=1, source_target_pairs={{0,8},{4,12},{8,0},{12,4},{16,24},{20,28},{24,16},{28,20},{1,9},{5... | collective-permute-start | bytes 559880 | tf_op jit(solution)/shard_map/ppermute | solution.py:136
  123.8 54.9 %collective-permute-start.6 = (bf16[1,144,648]{2,1,0:T(8,128)(2,1)S(1)}, bf16[1,144,648]{2,1,0:T(8,128)(2,1)S(1)}, u32[]{:S(2)}, u32[]{:S(2)}) collective-permute-start(bf16[1,144,648]{2,1,0:T(8,128)(2,1)S(1)} %get-tuple-element.40), channel_id=1, source_target_pairs={{0,28},{4,24},{8,20},{12,16},{16,12},{20,8},{24,4},{28,0},{1,29},{... | collective-permute-start | bytes 559880 | tf_op jit(solution)/shard_map/ppermute | solution.py:136
  126.2 52.5 %collective-permute-start.5 = (bf16[1,144,648]{2,1,0:T(8,128)(2,1)S(1)}, bf16[1,144,648]{2,1,0:T(8,128)(2,1)S(1)}, u32[]{:S(2)}, u32[]{:S(2)}) collective-permute-start(bf16[1,144,648]{2,1,0:T(8,128)(2,1)S(1)} %get-tuple-element.41), channel_id=1, source_target_pairs={{0,24},{4,28},{8,16},{12,20},{16,8},{20,12},{24,0},{28,4},{1,25},{... | collective-permute-start | bytes 559880 | tf_op jit(solution)/shard_map/ppermute | solution.py:136
  127.6 51.0 %collective-permute-start.4 = (bf16[1,144,648]{2,1,0:T(8,128)(2,1)S(1)}, bf16[1,144,648]{2,1,0:T(8,128)(2,1)S(1)}, u32[]{:S(2)}, u32[]{:S(2)}) collective-permute-start(bf16[1,144,648]{2,1,0:T(8,128)(2,1)S(1)} %get-tuple-element.42), channel_id=1, source_target_pairs={{0,20},{4,16},{8,28},{12,24},{16,4},{20,0},{24,12},{28,8},{1,21},{... | collective-permute-start | bytes 559880 | tf_op jit(solution)/shard_map/ppermute | solution.py:136
  129.1 24.8 %collective-permute-start.2 = (bf16[1,144,648]{2,1,0:T(8,128)(2,1)S(1)}, bf16[1,144,648]{2,1,0:T(8,128)(2,1)S(1)}, u32[]{:S(2)}, u32[]{:S(2)}) collective-permute-start(bf16[1,144,648]{2,1,0:T(8,128)(2,1)S(1)} %get-tuple-element.44), channel_id=1, source_target_pairs={{0,12},{4,8},{8,4},{12,0},{16,28},{20,24},{24,20},{28,16},{1,13},{... | collective-permute-start | bytes 559880 | tf_op jit(solution)/shard_map/ppermute | solution.py:136
  136.1 42.5 %collective-permute-start.3 = (bf16[1,144,648]{2,1,0:T(8,128)(2,1)S(1)}, bf16[1,144,648]{2,1,0:T(8,128)(2,1)S(1)}, u32[]{:S(2)}, u32[]{:S(2)}) collective-permute-start(bf16[1,144,648]{2,1,0:T(8,128)(2,1)S(1)} %get-tuple-element.43), channel_id=1, source_target_pairs={{0,16},{4,20},{8,24},{12,28},{16,0},{20,4},{24,8},{28,12},{1,17},{... | collective-permute-start | bytes 559880 | tf_op jit(solution)/shard_map/ppermute | solution.py:136
  188.3 103.2 %copy-start.22 = (bf16[192,1152]{1,0:T(8,128)(2,1)S(1)}, bf16[192,1152]{1,0:T(8,128)(2,1)}, u32[]{:S(2)}) copy-start(bf16[192,1152]{1,0:T(8,128)(2,1)} %param.18) | copy-start | bytes 1327108
  188.3 103.2 %copy-start.37 = (f32[48]{0:T(128)S(1)}, f32[48]{0:T(128)}, u32[]{:S(2)}) copy-start(f32[48]{0:T(128)} %copy-done.36) | copy-start | bytes 580
  188.3 165.6 %all-gather.7.cloned.1.call-start = ((), (), s32[]{:S(2)}) async-start(), calls=%async_computation.9 | async-start | bytes 3649536 | tf_op jit(solution)/shard_map/all_gather | solution.py:186
  189.1 169.9 %copy-start.31 = (f32[1152]{0:T(1024)}, f32[1152]{0:T(1024)S(1)}, u32[]{:S(2)}) copy-start(f32[1152]{0:T(1024)S(1)} %mul.587) | copy-start | bytes 13828
  291.5 67.5 %copy-start.58 = (f32[48]{0:T(128)}, f32[48]{0:T(128)S(1)}, u32[]{:S(2)}) copy-start(f32[48]{0:T(128)S(1)} %fusion.105) | copy-start | bytes 580
  294.8 171.3 %reduce-scatter.10.cloned.1.call-start = ((), (), s32[]{:S(2)}) async-start(), calls=%async_computation.10 | async-start | bytes 3649536 | tf_op jit(solution)/shard_map/reduce_scatter | solution.py:192
  364.2 101.9 %copy-start.4 = (bf16[48,1152]{1,0:T(8,128)(2,1)S(1)}, bf16[48,1152]{1,0:T(8,128)(2,1)}, u32[]{:S(2)}) copy-start(bf16[48,1152]{1,0:T(8,128)(2,1)} %reduce-scatter.6.cloned.1.call-done) | copy-start | bytes 331780
  364.2 101.9 %copy-start.38 = (f32[48]{0:T(128)S(1)}, f32[48]{0:T(128)}, u32[]{:S(2)}) copy-start(f32[48]{0:T(128)} %copy-done.36) | copy-start | bytes 580
  364.2 101.9 %copy-start.49 = (f32[48]{0:T(128)S(1)}, f32[48]{0:T(128)}, u32[]{:S(2)}) copy-start(f32[48]{0:T(128)} %copy-done.48) | copy-start | bytes 580
  364.2 101.9 %copy-start.57 = (f32[48]{0:T(128)S(1)}, f32[48]{0:T(128)}, u32[]{:S(2)}) copy-start(f32[48]{0:T(128)} %copy-done.56) | copy-start | bytes 580
  364.3 103.2 %copy-start.71 = (f32[48]{0:T(128)S(1)}, f32[48]{0:T(128)}, u32[]{:S(2)}) copy-start(f32[48]{0:T(128)} %copy-done.70) | copy-start | bytes 580
  364.3 103.2 %copy-start.12 = (bf16[48,1152]{1,0:T(8,128)(2,1)S(1)}, bf16[48,1152]{1,0:T(8,128)(2,1)}, u32[]{:S(2)}) copy-start(bf16[48,1152]{1,0:T(8,128)(2,1)} %reduce-scatter.8.cloned.1.call-done) | copy-start | bytes 331780
  364.3 103.2 %copy-start.32 = (f32[1152]{0:T(1024)S(1)}, f32[1152]{0:T(1024)}, u32[]{:S(2)}) copy-start(f32[1152]{0:T(1024)} %copy-done.31) | copy-start | bytes 13828
  364.3 103.2 %copy-start.59 = (f32[48]{0:T(128)S(1)}, f32[48]{0:T(128)}, u32[]{:S(2)}) copy-start(f32[48]{0:T(128)} %copy-done.58) | copy-start | bytes 580
  364.3 105.3 %copy-start.69 = (f32[48]{0:T(128)S(1)}, f32[48]{0:T(128)}, u32[]{:S(2)}) copy-start(f32[48]{0:T(128)} %copy-done.68) | copy-start | bytes 580
  364.3 112.2 %copy-start.6 = (bf16[8,144,1024]{2,1,0:T(8,128)(2,1)S(1)}, bf16[8,144,1024]{2,1,0:T(8,128)(2,1)}, u32[]{:S(2)}) copy-start(bf16[8,144,1024]{2,1,0:T(8,128)(2,1)} %copy-done.5) | copy-start | bytes 7077892
  364.3 136.3 %reduce-scatter.12.cloned.1.call-start = ((), (), s32[]{:S(2)}) async-start(), calls=%async_computation.11 | async-start | bytes 552960 | tf_op jit(solution)/shard_map/reduce_scatter | solution.py:221
  365.0 111.8 %copy-start.14 = (f32[192,192]{0,1:T(8,128)S(1)}, f32[192,192]{0,1:T(8,128)}, u32[]{:S(2)}) copy-start(f32[192,192]{0,1:T(8,128)} %copy-done.13) | copy-start | bytes 442372
  365.0 111.8 %copy-start.61 = (f32[192]{0:T(256)S(1)}, f32[192]{0:T(256)}, u32[]{:S(2)}) copy-start(f32[192]{0:T(256)} %copy-done.60) | copy-start | bytes 2308
  365.0 111.8 %copy-start.63 = (f32[192]{0:T(256)S(1)}, f32[192]{0:T(256)}, u32[]{:S(2)}) copy-start(f32[192]{0:T(256)} %copy-done.62) | copy-start | bytes 2308
  467.4 21.2 %copy-start.72 = (f32[48]{0:T(128)}, f32[48]{0:T(128)S(1)}, u32[]{:S(2)}) copy-start(f32[48]{0:T(128)S(1)} %get-tuple-element.29) | copy-start | bytes 580
  469.5 7.9 %copy-start.9 = (f32[48,1152]{1,0:T(8,128)}, f32[48,1152]{1,0:T(8,128)S(1)}, u32[]{:S(2)}) copy-start(f32[48,1152]{1,0:T(8,128)S(1)} %get-tuple-element.34) | copy-start | bytes 663556
  469.5 7.6 %copy-start.3 = (f32[192,768]{1,0:T(8,128)S(1)}, f32[192,768]{1,0:T(8,128)}, u32[]{:S(2)}) copy-start(f32[192,768]{1,0:T(8,128)} %copy-done.2) | copy-start | bytes 1769476
  480.5 129.3 %reduce-scatter.14.cloned.1.call-start = ((), (), s32[]{:S(2)}) async-start(), calls=%async_computation.12 | async-start | bytes 2949120 | tf_op jit(solution)/shard_map/reduce_scatter | solution.py:238
  503.9 3.6 copy-start.76
  503.9 137.9 %all-reduce.10.cloned.1.call-start = ((), (), s32[]{:S(2)}) async-start(), calls=%async_computation.13 | async-start | bytes 598016 | tf_op jit(solution)/shard_map/psum | solution.py:245
  592.7 8.2 %copy-start.73 = (f32[48]{0:T(128)S(1)}, f32[48]{0:T(128)}, u32[]{:S(2)}) copy-start(f32[48]{0:T(128)} %copy-done.72) | copy-start | bytes 580
  592.8 8.2 %copy-start.10 = (f32[48,1152]{1,0:T(8,128)S(1)}, f32[48,1152]{1,0:T(8,128)}, u32[]{:S(2)}) copy-start(f32[48,1152]{1,0:T(8,128)} %copy-done.9) | copy-start | bytes 663556
  592.8 8.2 %copy-start.18 = (bf16[48,1152]{1,0:T(8,128)(2,1)S(1)}, bf16[48,1152]{1,0:T(8,128)(2,1)}, u32[]{:S(2)}) copy-start(bf16[48,1152]{1,0:T(8,128)(2,1)} %reduce-scatter.12.cloned.1.call-done) | copy-start | bytes 331780
  (46 other events, 62.7 us)
Sparse Core Ops, SparseCore 0:
  13.2 57.3 all-gather.8
  79.8 19.6 reduce-scatter.5
  104.1 74.8 all-gather.4
  188.4 101.9 reduce-scatter.7
  295.0 58.9 all-gather.6
  364.5 101.6 reduce-scatter.9
  480.6 20.0 reduce-scatter.11
  504.2 93.0 reduce-scatter.13
  611.8 29.9 all-reduce.9
